TPU v7x, 128 devices: a whole 4x4x4 slice. The times are simulated.
128 devices in a mesh: row: 16 (over y, x), col: 8 (over z, core).
Axes of the slice: x: 4, y: 4, z: 4, core: 2. Of those that a mesh axis runs over, the one named last changes fastest.
Arguments:
- upper_block: float32 [2, 1024, 1024], P(None, 'row', 'col'), may hold values from -0.25 to 0.25
- block_inverse: float32 [2, 1024, 64], P(None, 'row'), may hold values from -0.375 to 0.375
- panel_rhs: float32 [2, 32, 1024], P(None, None, 'row'), may hold values from -6 to 6
- upper_trail: float32 [2, 1024, 131072], P(None, 'row', 'col'), may hold values from -0.125 to 0.125
- trail_rhs: float32 [2, 32, 131072], P(None, None, ('col', 'row')), may hold values from -6 to 6
- currents: float32 [2, 1024], P(None, 'row'), may hold values from -4 to 4
- owner: int32 [1024], P('row'), may hold values from 0 to 511
Outputs:
- panel_adjoint: float32 [2, 32, 1024], P(None, None, 'row')
- trail_updated: float32 [2, 32, 131072], P(None, None, ('col', 'row'))
- patch_gradient: float32 [512], P(('row', 'col'))
Inputs may be any that keep to these rules, and one draw needn't show every extreme that they name: owner names a surface patch for each panel unknown.
All inputs are finite; a program needn't handle non-finite values.
Results may differ from a plain program's by a relative error of at most 0.0003.
Values sent between devices are 32-bit elements; how exact they have to be, the bound alone decides.
A program may use at most 64 MiB of HBM per device.

v0:
```python
import jax
import jax.numpy as jnp
from jax import lax
from jax.sharding import Mesh
from jax.sharding import PartitionSpec as P

PATCH_DEV = 4
ROW = ("row_0", "row_1")
ROW_COL = ("row_0", "row_1", "col")
COL_ROW = ("col", "row_0", "row_1")


highest = lax.Precision.HIGHEST


def rows_first(arrays, axis, dims):
    turned = [jnp.moveaxis(a, dim, 0) for a, dim in zip(arrays, dims)]
    widths = [t[0].size for t in turned]
    both = jnp.concatenate([t.reshape(-1, w) for t, w in zip(turned, widths)], axis=1)
    filled = lax.all_gather(both, axis, axis=0, tiled=True)
    pieces = jnp.split(filled, [sum(widths[:k]) for k in range(1, len(widths))], axis=1)
    return tuple(
        (
            jnp.moveaxis(b.reshape(-1, *t.shape[1:]), 0, dim)
            for b, t, dim in zip(pieces, turned, dims)
        )
    )


def sum_by_axis(value, axes, dim):
    if not axes:
        return value
    nearer = lax.psum_scatter(value, axes[0], scatter_dimension=dim, tiled=True)
    return sum_by_axis(nearer, axes[1:], dim)


def product_high(first, second):
    return jnp.dot(first, second, precision=highest, preferred_element_type=jnp.float32)


def conj_product(left, right):
    real_part = product_high(left[0], right[0]) + product_high(left[1], right[1])
    imag_part = product_high(left[1], right[0]) - product_high(left[0], right[1])
    return jnp.stack([real_part, imag_part])


def sweep(upper, inverses, rhs, width):
    count = rhs.shape[2] // width
    held_start = jnp.zeros(rhs.shape, jnp.float32)
    solved_start = jnp.zeros(rhs.shape, jnp.float32)

    def advance(index, carry):
        held, solved = carry
        start = (jnp.asarray(index) * width).astype(jnp.int32)
        local = lax.dynamic_slice_in_dim(held, start, width, 2)
        residual = lax.dynamic_slice_in_dim(rhs, start, width, 2) - local
        inverse = lax.dynamic_slice_in_dim(inverses, start, width, 1)
        value = conj_product(residual, inverse)
        rows_here = lax.dynamic_slice_in_dim(upper, start, width, 1)
        held = held + conj_product(value, rows_here)
        solved = lax.dynamic_update_slice_in_dim(solved, value, start, 2)
        return (held, solved)

    return lax.fori_loop(0, count, advance, (held_start, solved_start))[1]


def on_device(upper_block, block_inverse, panel_rhs, upper_trail, trail_rhs, currents, owner):
    rows_count = lax.axis_size(ROW)
    cols_count = lax.axis_size("col")
    row_index = lax.axis_index(ROW)
    col_index = lax.axis_index("col")
    width = block_inverse.shape[1]
    whole_rows, inverses, rhs_all = rows_first(
        (upper_block, block_inverse, panel_rhs), ROW, (1, 1, 2)
    )
    whole = lax.all_gather(whole_rows, "col", axis=2, tiled=True)
    solved_all = sweep(whole, inverses, rhs_all, width)
    solved = lax.dynamic_slice_in_dim(solved_all, row_index * width, width, 2)
    term = conj_product(solved, upper_trail)
    reduced = sum_by_axis(term, ROW, 2)
    updated = trail_rhs - reduced
    share = width // cols_count
    start = col_index * share
    mine = lax.dynamic_slice_in_dim(solved, start, share, 2)
    total = jnp.sum(mine, axis=1)
    current_part = lax.dynamic_slice_in_dim(currents, start, share, 1)
    owner_part = lax.dynamic_slice_in_dim(owner, start, share, 0)
    partial_value = current_part[0] * total[0] - current_part[1] * total[1]
    patch_count = PATCH_DEV * rows_count * cols_count
    patch_ids = lax.broadcasted_iota(jnp.int32, (share, patch_count), 1)
    selector = (owner_part[:, None] == patch_ids).astype(jnp.float32)
    spread = product_high(partial_value[None, :], selector)[0]
    gradient = lax.psum_scatter(spread, ROW_COL, scatter_dimension=0, tiled=True)
    return (solved, updated, gradient)


def solution(mesh):
    split = Mesh(mesh.devices.reshape(4, 4, mesh.shape["col"]), ("row_0", "row_1", "col"))
    return jax.shard_map(
        on_device,
        mesh=split,
        in_specs=(
            P(None, ROW, "col"),
            P(None, ROW, None),
            P(None, None, ROW),
            P(None, ROW, "col"),
            P(None, None, COL_ROW),
            P(None, ROW),
            P(ROW),
        ),
        out_specs=(P(None, None, ROW), P(None, None, COL_ROW), P(ROW_COL)),
        check_vma=False,
    )
```

profile of v0, /device:TPU:0, one launch (start us, length us, event | category | flops | bytes accessed | tf_op | source)
XLA Modules:
  0.0 363.8 jit_solution(3339413474390331940)
XLA Ops:
  9.8 48.2 %all-gather.3.cloned.1.call-done = f32[1024,448]{1,0:T(8,128)} async-done(((f32[64,448]{1,0:T(8,128)}), f32[1024,448]{1,0:T(8,128)}) %all-gather.3.cloned.1.call-update) | async-done | bytes 1835024 | tf_op jit(solution)/shard_map/all_gather | solution.py:20
  58.0 1.4 split.14
  59.4 1.3 copy.31
  61.2 49.0 %all-gather.5.cloned.1.call-done = f32[2,1024,1024]{1,2,0:T(8,128)} async-done(((f32[2,1024,128]{1,2,0:T(8,128)}), f32[2,1024,1024]{1,2,0:T(8,128)}) %all-gather.5.cloned.1.call-update) | async-done | bytes 8388624 | tf_op jit(solution)/shard_map/all_gather | solution.py:76
  110.2 8.7 %copy.33 = f32[2,1024,1024]{2,1,0:T(8,128)} copy(f32[2,1024,1024]{1,2,0:T(8,128)} %all-gather.5.cloned.1.call-done) | data formatting | bytes 16777216
  118.9 106.3 %while.16 = (s32[]{:T(128)}, f32[2,32,1024]{2,1,0:T(8,128)S(1)}, f32[2,32,1024]{2,1,0:T(8,128)S(1)}, f32[2,32,1024]{2,1,0:T(8,128)S(1)}, f32[2,1024,64]{1,2,0:T(...) while((s32[]{:T(128)}, f32[2,32,1024]{2,1,0:T(8,128)S(1)}, ...), condition=%wide.region_1.0_spmd.clone, body=%wide.region_0.0_spmd.clone.sunk | while | flops 107294728 | bytes 3555570 | solution.py:64
  119.6 1.2 fusion.58
  121.3 1.2 fusion.60
  123.8 1.2 fusion.62
  126.1 1.2 fusion.58
  127.8 1.2 fusion.60
  130.3 1.2 fusion.62
  132.9 1.2 fusion.58
  134.6 1.2 fusion.60
  137.1 1.2 fusion.62
  139.4 1.2 fusion.58
  141.1 1.2 fusion.60
  143.6 1.2 fusion.62
  146.2 1.2 fusion.58
  147.9 1.2 fusion.60
  150.4 1.2 fusion.62
  152.7 1.2 fusion.58
  154.4 1.2 fusion.60
  155.7 1.2 fusion.61
  156.9 1.2 fusion.62
  159.5 1.2 fusion.58
  161.2 1.2 fusion.60
  163.7 1.2 fusion.62
  166.0 1.2 fusion.58
  167.7 1.2 fusion.60
  170.2 1.2 fusion.62
  172.8 1.2 fusion.58
  174.5 1.2 fusion.60
  175.8 1.2 fusion.61
  177.0 1.2 fusion.62
  179.3 1.2 fusion.58
  181.1 1.2 fusion.60
  183.5 1.2 fusion.62
  186.1 1.2 fusion.58
  187.8 1.2 fusion.60
  190.3 1.2 fusion.62
  192.6 1.2 fusion.58
  194.4 1.2 fusion.60
  196.8 1.2 fusion.62
  199.4 1.2 fusion.58
  201.2 1.2 fusion.60
  203.6 1.2 fusion.62
  205.9 1.2 fusion.58
  207.7 1.2 fusion.60
  210.1 1.2 fusion.62
  212.7 1.2 fusion.58
  214.5 1.2 fusion.60
  216.9 1.2 fusion.62
  219.2 1.2 fusion.58
  220.9 1.2 fusion.60
  223.3 1.2 fusion.62
  225.2 4.0 %fusion.20 = f32[32,16384]{1,0:T(8,128)S(1)} fusion(f32[2,64,16384]{2,1,0:T(8,128)} %param.12, f32[2,32,1024]{2,1,0:T(8,128)S(1)} %get-tuple-element.112, s32[]{:T(128)S(6)} %select_n.23), kind=kOutput, calls=%fused_computation.37 | convolution fusion | flops 402653184 | bytes 6307844 | tf_op jit(solution)/shard_map/dot_general | solution.py:38
  229.3 4.1 %fusion.18 = f32[32,16384]{1,0:T(8,128)S(1)} fusion(f32[2,64,16384]{2,1,0:T(8,128)} %param.12, f32[2,32,1024]{2,1,0:T(8,128)S(1)} %get-tuple-element.112, s32[]{:T(128)S(6)} %add.84, s32[]{:T(128)S(6)} %select_n.23), kind=kOutput, calls=%fused_computation.35 | convolution fusion | flops 402653184 | bytes 6307848 | tf_op jit(solution)/shard_map/dot_general | solution.py:38
  233.4 3.9 %fusion.14 = f32[1,32,16384]{2,1,0:T(8,128)S(1)} fusion(f32[32,16384]{1,0:T(8,128)S(1)} %fusion.18, f32[2,64,16384]{2,1,0:T(8,128)} %param.12, f32[2,32,1024]{2,1,0:T(8,128)S(1)} %get-tuple-element.112, s32[]{:T(128)S(6)} %select_n.23), kind=kOutput, calls=%fused_computation.29 | convolution fusion | flops 403177472 | bytes 8404996 | tf_op jit(solution)/shard_map/dot_general | solution.py:38
  237.3 2.2 fusion.15
  239.5 2.2 pad_maximum_fusion.1
  241.8 47.0 %reduce-scatter.3.cloned.1.call-done = f32[2,32,4096]{2,1,0:T(8,128)} async-done(((f32[2,32,16384]{2,1,0:T(8,128)}), f32[2,32,4096]{2,1,0:T(8,128)}) %reduce-scatter.3.cloned.1.call-update) | async-done | bytes 1048592 | tf_op jit(solution)/shard_map/reduce_scatter | solution.py:33
  289.3 65.0 %all-reduce = f32[512]{0:T(512)S(1)} all-reduce(f32[512]{0:T(512)S(1)} %bitcast.133), channel_id=4, replica_groups=mesh['row_0'=4,'row_1'=4,'col'=8] {'row_0','row_1','col'}, use_global_device_ids=true, to_apply=%region_5.0.clone | all-reduce | flops 512 | bytes 4096
  355.6 1.7 sub.32
  (199 shorter events, 48.1 us)
Async XLA Ops:
  7.2 1.9 copy-start
  7.2 50.8 %all-gather.3.cloned.1.call-start = ((), (), s32[]{:S(2)}) async-start(), calls=%async_computation.2 | async-start | bytes 2228224 | tf_op jit(solution)/shard_map/all_gather | solution.py:20
  9.8 100.5 %all-gather.5.cloned.1.call-start = ((), (), s32[]{:S(2)}) async-start(), calls=%async_computation.3 | async-start | bytes 9437184 | tf_op jit(solution)/shard_map/all_gather | solution.py:76
  58.0 2.8 slice-start.2
  58.0 3.0 slice-start.3
  60.8 228.0 %reduce-scatter.3.cloned.1.call-start = ((), (), s32[]{:S(2)}) async-start(), calls=%async_computation.4 | async-start | bytes 5242880 | tf_op jit(solution)/shard_map/reduce_scatter | solution.py:33
  225.2 12.1 %slice-start = ((s8[8388608]{0:T(1024)(128)(4,1)}), s8[4194304]{0:T(1024)(128)(4,1)S(1)}, s32[]{:S(2)}) async-start(s8[8388608]{0:T(1024)(128)(4,1)} %bitcast.124), calls=%async_computation.6 | async-start | bytes 8388608
  229.3 8.0 %slice-start.1 = ((s8[8388608]{0:T(1024)(128)(4,1)}), s8[4194304]{0:T(1024)(128)(4,1)S(1)}, s32[]{:S(2)}) async-start(s8[8388608]{0:T(1024)(128)(4,1)} %bitcast.124), calls=%async_computation.7 | async-start | bytes 8388608
  241.8 47.1 %copy-start.3 = (s32[64]{0:T(128)S(1)}, s32[64]{0:T(128)}, u32[]{:S(2)}) copy-start(s32[64]{0:T(128)} %param.15) | copy-start | bytes 772
  241.8 47.2 %copy-start.2 = (f32[2,64]{1,0:T(2,128)S(1)}, f32[2,64]{1,0:T(2,128)}, u32[]{:S(2)}) copy-start(f32[2,64]{1,0:T(2,128)} %param.14) | copy-start | bytes 1540
  241.8 113.8 %copy-start.1 = (f32[2,32,1024]{2,1,0:T(8,128)S(1)}, f32[2,32,1024]{2,1,0:T(8,128)}, u32[]{:S(2)}) copy-start(f32[2,32,1024]{2,1,0:T(8,128)} %param.13) | copy-start | bytes 786436
  241.8 113.8 %reduce-scatter.5.cloned.1.call-start = ((), (), s32[]{:S(2)}) async-start(), calls=%async_computation.5 | async-start | bytes 1310720 | tf_op jit(solution)/shard_map/reduce_scatter | solution.py:33
Sparse Core Ops, SparseCore 0:
  10.7 47.2 all-gather.2
  60.9 49.3 all-gather.4
  241.9 46.8 reduce-scatter.2
  291.2 23.2 reduce-scatter.4
where the time goes:
time: 367 us; the launch traced here: 364 us
  waiting for transfers between devices  144 us (39%)
  matrix products  108 us (29%)
  blocking collectives  65 us (18%)
  local copies, waits for them, and re-layouts  22.7 us (6%)
  between operations  13.9 us (4%)
  other arithmetic  7.86 us (2%)
    dot_general x133, matrix products, product_high(): jnp.dot(first, second, precision=highest, preferred_element_type=jnp.floa...  108 us
    unnamed x1, blocking collectives  65 us
    all_gather x1, waiting for transfers between devices, on_device(): whole = lax.all_gather(whole_rows, 'col', axis=2, tiled=True)  49 us
    all_gather x1, waiting for transfers between devices, rows_first(): filled = lax.all_gather(both, axis, axis=0, tiled=True)  48.2 us
    reduce_scatter x2, waiting for transfers between devices, sum_by_axis(): nearer = lax.psum_scatter(value, axes[0], scatter_dimension=dim, tiled=True)  47 us
    unnamed x14, local copies, waits for them, and re-layouts  9.29 us
    dynamic_update_slice x16, local copies, waits for them, and re-layouts, advance(): solved = lax.dynamic_update_slice_in_dim(solved, value, start, 2)  7.65 us
  transfers between devices with their start and end apart: 4, of which 3 were waited for; matrix products, arithmetic and copies ran while one was open for 1% of the time, Pallas kernels for 0%

commit v1 on v0

v1 whole, which is shorter than its diff:
```python
import jax
import jax.numpy as jnp
from jax import lax
from jax.experimental import pallas as pl
from jax.experimental.pallas import tpu as pltpu
from jax.sharding import PartitionSpec as P

MESH = pl.DeviceIdType.MESH
F32 = jnp.float32
BF16 = jnp.bfloat16
Y, X, Z = 0, 1, 2
DISTS = (1, 3, 2)
ORDER = (2, 1, 3, 0)


def halves(value):
    high = value.astype(BF16)
    low = (value - high.astype(F32)).astype(BF16)
    return high, low


def stacked(value):
    high, low = halves(value)
    return jnp.concatenate([high, low], axis=0)


def left_side(value):
    high, low = halves(value)
    both = jnp.concatenate([high, low], axis=0)
    return jnp.concatenate([both, both], axis=1)


def multiply(left, right):
    out = jnp.dot(left, right, preferred_element_type=F32)
    rows = out.shape[0] // 2
    return out[:rows] + out[rows:]


def conj_left(value):
    re, im = value[:, :64], value[:, 64:]
    turned = jnp.concatenate([im, -re], axis=1)
    return left_side(jnp.concatenate([value, turned], axis=0))


class Message:
    def __init__(self, where, cond, dim, dist, send, recv):
        self.where, self.cond, self.dim, self.dist = where, cond, dim, dist
        self.send, self.recv = send, recv


def body(
    upper_ref, inverse_ref, rhs_ref, trail_hbm, trail_rhs_hbm, currents_ref, owner_ref,
    solved_ref, updated_ref, gradient_ref,
    pieces, rhs_all, held, answers, trail, trail_rhs,
    first_out, first_in, second_out, second_in, third_out, third_in, fourth_in, tiles,
    local_sem, g_send, g_recv, k_send, k_recv, r_send, r_recv, t_send, t_recv,
):
    row, col = lax.axis_index("row"), lax.axis_index("col")
    me = (row // 4, row % 4, col // 2)
    core = col % 2

    def shifted(coords, dim, dist):
        moved = list(coords)
        moved[dim] = (moved[dim] + dist) % 4
        return tuple(moved)

    def device(coords, which):
        return (coords[0] * 4 + coords[1], coords[2] * 2 + which)

    def peer(dim, dist):
        if dim is None:
            return device(me, 1 - core)
        return device(shifted(me, dim, dist), core)

    loads = []
    for part in range(4):
        cols = pl.ds(part * 4096, 4096)
        loads.append(pltpu.make_async_copy(trail_hbm.at[:, :, cols], trail.at[:, :, cols], local_sem.at[part]))
    loads.append(pltpu.make_async_copy(trail_rhs_hbm, trail_rhs, local_sem.at[4]))
    for load in loads:
        load.start()

    barrier = pltpu.get_barrier_semaphore()
    for dim in (Y, X, Z):
        for dist in DISTS:
            pl.semaphore_signal(barrier, inc=1, device_id=peer(dim, dist), device_id_type=MESH)
    pl.semaphore_signal(barrier, inc=1, device_id=peer(None, 0), device_id_type=MESH)

    upper = upper_ref[...].reshape(128, 128)
    inv_re, inv_im = inverse_ref[0], inverse_ref[1]
    left = jnp.concatenate(
        [jnp.concatenate([inv_re, -inv_im], axis=1), jnp.concatenate([inv_im, inv_re], axis=1)], axis=0
    )
    pieces[me[0], me[1], me[2], core] = multiply(left_side(left), stacked(upper))
    rhs_all[me[0], me[1]] = jnp.concatenate([rhs_ref[0], rhs_ref[1]], axis=1)

    pl.semaphore_wait(barrier, 10)

    def copy_of(message, coords):
        ref = message.where(coords)
        return pltpu.make_async_remote_copy(
            src_ref=ref, dst_ref=ref, send_sem=message.send, recv_sem=message.recv,
            device_id=peer(message.dim, message.dist), device_id_type=MESH,
        )

    def guarded(cond, action):
        if cond is True:
            action()
        else:
            pl.when(cond)(action)

    def start(message):
        guarded(message.cond(me), lambda: copy_of(message, me).start())

    def source(message):
        return me if message.dim is None else shifted(me, message.dim, -message.dist + 4)

    def arrived(message):
        coords = source(message)
        guarded(message.cond(coords), lambda: copy_of(message, coords).wait_recv())

    def sent(message):
        guarded(message.cond(me), lambda: copy_of(message, me).wait_send())

    count = [0]
    forwards = []

    def message(where, cond, dim, dist):
        slot = count[0]
        count[0] += 1
        return Message(where, cond, dim, dist, g_send.at[slot], g_recv.at[slot])

    def forward(received):
        slot = len(forwards)
        coords = source(received)
        cond = received.cond(coords)

        def make(which):
            ref = received.where(coords, which)
            return pltpu.make_async_remote_copy(
                src_ref=ref, dst_ref=ref, send_sem=k_send.at[slot], recv_sem=k_recv.at[slot],
                device_id=peer(None, 0), device_id_type=MESH,
            )

        guarded(cond, lambda: make(core).start())
        forwards.append((cond, make))

    always = lambda c: True
    upper_half = lambda c: c[0] <= c[2]

    def stage_messages(rows, dims, groups):
        out = []
        for dim, group in zip(dims, groups):
            stage = []
            for dist in DISTS:
                for where, cond in group:
                    stage.append(message(where, cond, dim, dist))
            out.append(stage)
        return out

    def own(rows):
        return [(lambda c, k=core: pieces.at[c[0], c[1], c[2], k, rows], upper_half)]

    rows_a, rows_b, rows_c = pl.ds(0, 64), pl.ds(64, 32), pl.ds(96, 32)
    part_a = stage_messages(rows_a, (Z, Y, X), [
        own(rows_a),
        [(lambda c, k=core, z=z: pieces.at[c[0], c[1], z, k, rows_a], lambda c, z=z: c[0] <= z) for z in range(4)],
        [(lambda c, k=core, y=y: pieces.at[y, c[1], pl.ds(y, 4 - y), k, rows_a], always) for y in range(4)],
    ])
    part_b = stage_messages(rows_b, (X, Z, Y), [
        own(rows_b),
        [(lambda c, k=core: pieces.at[c[0], :, c[2], k, rows_b], upper_half)],
        [(lambda c, k=core, z=z: pieces.at[c[0], :, z, k, rows_b], lambda c, z=z: c[0] <= z) for z in range(4)],
    ])
    part_c = stage_messages(rows_c, (Y, X, Z), [
        own(rows_c),
        [(lambda c, k=core, y=y: pieces.at[y, c[1], c[2], k, rows_c], lambda c, y=y: y <= c[2]) for y in range(4)],
        [(lambda c, k=core, y=y: pieces.at[y, :, c[2], k, rows_c], lambda c, y=y: y <= c[2]) for y in range(4)],
    ])

    def half_rhs(c, k=core):
        return rhs_all.at[c[0], c[1], pl.ds(pl.multiple_of(k * 16, 16), 16)]

    def half_rhs_row(c, k=core):
        return rhs_all.at[c[0], :, pl.ds(pl.multiple_of(k * 16, 16), 16)]

    part_r = stage_messages(None, (X, Y), [[(half_rhs, always)], [(half_rhs_row, always)]])

    mine = Message(lambda c, k=core: pieces.at[c[0], c[1], c[2], k], upper_half, None, 0, None, None)
    stages = [
        part_r[0] + part_a[0] + part_b[0] + part_c[0],
        part_r[1] + part_a[1] + part_b[1] + part_c[1],
        part_a[2] + part_b[2] + part_c[2],
    ]
    for number, stage in enumerate(stages):
        for item in stage:
            start(item)
        if number == 0:
            forward(mine)
        interleaved = sorted(range(len(stage)), key=lambda i: DISTS.index(stage[i].dist))
        for i in interleaved:
            arrived(stage[i])
            forward(stage[i])
    for cond, make in forwards:
        guarded(cond, lambda make=make: make(1 - core).wait_recv())

    held[...] = jnp.zeros_like(held)
    lanes = lax.broadcasted_iota(jnp.int32, (32, 128), 1)
    for k in range(16):
        tile = held[:, (k // 2) * 128:(k // 2 + 1) * 128]
        if k % 2 == 0:
            local = jnp.where(lanes < 64, tile[:32], pltpu.roll(tile[32:], 64, 1))
        else:
            local = jnp.where(lanes < 64, pltpu.roll(tile[:32], 64, 1), tile[32:])
        value = rhs_all[k // 4, k % 4] - local
        answers[k] = value
        first = (k + 1) // 2
        if first < 8:
            lhs = conj_left(value)
            for c in range(first, 8):
                rhs = stacked(pieces[k // 4, k % 4, c // 2, c % 2])
                held[:, c * 128:(c + 1) * 128] += multiply(lhs, rhs)

    value = multiply(conj_left(answers[row]), stacked(inverse_ref[...].reshape(128, 64)))
    solved_ref[...] = value.reshape(2, 32, 64)
    lhs = conj_left(jnp.concatenate([value[:32], value[32:]], axis=1))

    total_re = jnp.sum(value[:32], axis=0, keepdims=True)
    total_im = jnp.sum(value[32:], axis=0, keepdims=True)
    partial_value = currents_ref[0:1, :] * total_re - currents_ref[1:2, :] * total_im
    tiles[me[0], me[1], 0:1, 0:64] = partial_value
    tiles[me[0], me[1], 1:2, 0:64] = owner_ref[...].astype(F32)
    tiles[me[0], me[1], 0:2, 64:128] = jnp.full((2, 64), -1.0, F32)
    tiles[me[0], me[1], 2:8, :] = jnp.zeros((6, 128), F32)
    tile_messages = []
    for n, (dim, where) in enumerate(((X, lambda c: tiles.at[c[0], c[1]]), (Y, lambda c: tiles.at[c[0]]))):
        tile_messages.append([Message(where, always, dim, d, t_send.at[n, i], t_recv.at[n, i]) for i, d in enumerate(DISTS)])
    for item in tile_messages[0]:
        start(item)

    for load in loads:
        load.wait()

    def term(half, a, j):
        dims = (X, Y) if half == 0 else (Y, X)
        there = shifted(shifted(me, dims[0], a), dims[1], j)
        begin = pl.multiple_of((there[0] * 4 + there[1]) * 1024 + half * 512, 512)
        block = trail[:, :, pl.ds(begin, 512)].reshape(128, 512)
        return multiply(lhs, stacked(block))

    def send(src, dst, dim, dist, slot):
        copy = pltpu.make_async_remote_copy(
            src_ref=src, dst_ref=dst, send_sem=r_send.at[slot], recv_sem=r_recv.at[slot],
            device_id=peer(dim, dist), device_id_type=MESH,
        )
        copy.start()
        return copy

    DIM = ((X, Y), (Y, X))
    top, low = pl.ds(0, 32), pl.ds(32, 32)
    one, two, three, four = {}, {}, {}, {}
    for n, j in enumerate(ORDER):
        for h in range(2):
            first_out[h, n] = term(h, 2, j)
            slot = (h * 4 + n) * 2
            one[h, n, 0] = send(first_out.at[h, n, top], first_in.at[h, n, 0], DIM[h][0], 1, slot)
            one[h, n, 1] = send(first_out.at[h, n, low], first_in.at[h, n, 1], DIM[h][0], 3, slot + 1)
        if n == 0:
            for item in tile_messages[0]:
                arrived(item)
            for item in tile_messages[1]:
                start(item)
    for n, j in enumerate(ORDER):
        for h in range(2):
            slot = 16 + (h * 4 + n) * 2
            for s, a in enumerate((1, 3)):
                second_out[h, n, s] = term(h, a, j)
                one[h, n, s].wait_recv()
                rows = top if s == 0 else low
                second_out[h, n, s, rows] += first_in[h, n, s]
                two[h, n, s] = send(second_out.at[h, n, s], second_in.at[h, n, s], DIM[h][0], a, slot + s)
    for n, j in enumerate(ORDER):
        for h in range(2):
            third_out[h, n] = term(h, 0, j)
            for s in range(2):
                two[h, n, s].wait_recv()
            third_out[h, n] += second_in[h, n, 0] + second_in[h, n, 1]
            if j == 2:
                three[h, 0] = send(third_out.at[h, n, top], third_in.at[h, 0], DIM[h][1], 1, 32 + h * 4)
                three[h, 1] = send(third_out.at[h, n, low], third_in.at[h, 1], DIM[h][1], 3, 33 + h * 4)
            elif j == 0:
                for s in range(2):
                    four[h, s].wait_recv()
                total = third_out[h, n] + fourth_in[h, 0] + fourth_in[h, 1]
                cols = pl.ds(h * 512, 512)
                updated_ref[:, :, cols] = trail_rhs[:, :, cols] - total.reshape(2, 32, 512)
            else:
                s = 0 if j == 1 else 1
                rows = top if s == 0 else low
                three[h, s].wait_recv()
                third_out[h, n, rows] += third_in[h, s]
                four[h, s] = send(third_out.at[h, n], fourth_in.at[h, s], DIM[h][1], j, 34 + h * 4 + s)

    for item in tile_messages[1]:
        arrived(item)
    parts = tiles[...].reshape(16, 8, 128)
    for n in range(4):
        patch = ((row * 8 + col) * 4 + n).astype(F32)
        chosen = jnp.where(parts[:, 1, :] == patch, parts[:, 0, :], 0.0)
        gradient_ref[n] = jnp.sum(chosen)

    for stage in stages:
        for item in stage:
            sent(item)
    for cond, make in forwards:
        guarded(cond, lambda make=make: make(core).wait_send())
    for group in tile_messages:
        for item in group:
            sent(item)
    for group in (one, two, three, four):
        for copy in group.values():
            copy.wait_send()


def on_device(upper_block, block_inverse, panel_rhs, upper_trail, trail_rhs, currents, owner):
    vmem = pl.BlockSpec(memory_space=pltpu.VMEM)
    anywhere = pl.BlockSpec(memory_space=pl.ANY)
    dma = pltpu.SemaphoreType.DMA
    return pl.pallas_call(
        body,
        out_shape=(
            jax.ShapeDtypeStruct((2, 32, 64), F32),
            jax.ShapeDtypeStruct((2, 32, 1024), F32),
            jax.ShapeDtypeStruct((4,), F32),
        ),
        in_specs=[vmem, vmem, vmem, anywhere, anywhere, vmem, vmem],
        out_specs=(vmem, vmem, pl.BlockSpec(memory_space=pltpu.SMEM)),
        scratch_shapes=[
            pltpu.VMEM((4, 4, 4, 2, 128, 128), F32),
            pltpu.VMEM((4, 4, 32, 128), F32),
            pltpu.VMEM((64, 1024), F32),
            pltpu.VMEM((16, 32, 128), F32),
            pltpu.VMEM((2, 64, 16384), F32),
            pltpu.VMEM((2, 32, 1024), F32),
            pltpu.VMEM((2, 4, 64, 512), F32),
            pltpu.VMEM((2, 4, 2, 32, 512), F32),
            pltpu.VMEM((2, 4, 2, 64, 512), F32),
            pltpu.VMEM((2, 4, 2, 64, 512), F32),
            pltpu.VMEM((2, 4, 64, 512), F32),
            pltpu.VMEM((2, 2, 32, 512), F32),
            pltpu.VMEM((2, 2, 64, 512), F32),
            pltpu.VMEM((4, 4, 8, 128), F32),
            dma((5,)),
            dma((80,)), dma((80,)),
            dma((80,)), dma((80,)),
            dma((40,)), dma((40,)),
            dma((2, 3)), dma((2, 3)),
        ],
        compiler_params=pltpu.CompilerParams(
            collective_id=0, has_side_effects=True, vmem_limit_bytes=48 * 2**20
        ),
        name="panel",
    )(upper_block, block_inverse, panel_rhs, upper_trail, trail_rhs, currents, owner.reshape(1, 64))


def solution(mesh):
    return jax.shard_map(
        on_device,
        mesh=mesh,
        in_specs=(
            P(None, "row", "col"),
            P(None, "row", None),
            P(None, None, "row"),
            P(None, "row", "col"),
            P(None, None, ("col", "row")),
            P(None, "row"),
            P("row"),
        ),
        out_specs=(P(None, None, "row"), P(None, None, ("col", "row")), P(("row", "col"))),
        check_vma=False,
    )
```

time: 367 us -> 80.1 us (0.22)
  waiting for transfers between devices: 144 us -> 0 us
  matrix products: 108 us -> 0 us
  Pallas kernels: 0 us -> 71.7 us
  blocking collectives: 65 us -> 0 us
  local copies, waits for them, and re-layouts: 22.7 us -> 6.54 us
  between operations: 13.9 us -> 0.66 us
  other arithmetic: 7.86 us -> 0 us
    dot_general x133 -> x0, matrix products: 108 us -> none  [product_high(): jnp.dot(first, second, precision=highest, preferred_element_type=jnp.floa...]
    all_gather x2 -> x0, waiting for transfers between devices: 97.2 us -> none  [the longest x1 49 us: on_device(): whole = lax.all_gather(whole_rows, 'col', axis=2, tiled=True)]
    pallas_call x0 -> x1, Pallas kernels: none -> 71.7 us  [on_device(): pl.pallas_call(body, out_shape=(jax.ShapeDtypeStruct((2, 32, 64), F32), j...]
    unnamed x1 -> x0, blocking collectives: 65 us -> none
    reduce_scatter x2 -> x0, waiting for transfers between devices: 47 us -> none  [sum_by_axis(): nearer = lax.psum_scatter(value, axes[0], scatter_dimension=dim, tiled=True)]
    dynamic_update_slice x16 -> x0, local copies, waits for them, and re-layouts: 7.65 us -> none  [advance(): solved = lax.dynamic_update_slice_in_dim(solved, value, start, 2)]
    unnamed x14 -> x15, local copies, waits for them, and re-layouts: 9.29 us -> 6.54 us
  transfers between devices with their start and end apart: 4 -> 0, of which waited for: 3 -> 0; matrix products, arithmetic and copies ran while one was open for 1% -> 0% of each run, Pallas kernels for 0% -> 0%
where the time goes in v1:
time: 80.1 us; the launch traced here: 78.9 us
  Pallas kernels  71.7 us (90%)
  local copies, waits for them, and re-layouts  6.54 us (8%)
    pallas_call x1, Pallas kernels, on_device(): pl.pallas_call(body, out_shape=(jax.ShapeDtypeStruct((2, 32, 64), F32), j...  71.7 us
    unnamed x15, local copies, waits for them, and re-layouts  6.54 us

profile of v1, /device:TPU:0, one launch (start us, length us, event | category | flops | bytes accessed | tf_op | source)
XLA Modules:
  0.0 78.9 jit_solution(4694501555777397379)
XLA Ops:
  0.6 0.0 copy-start
  0.6 0.9 %copy-done = f32[2,32,1024]{2,1,0:T(8,128)S(1)} copy-done((f32[2,32,1024]{2,1,0:T(8,128)S(1)}, f32[2,32,1024]{2,1,0:T(8,128)}, u32[]{:S(2)}) %copy-start) | copy-done | bytes 262168
  1.6 0.0 copy-start.1
  1.6 0.8 %copy-done.1 = f32[2,64,128]{2,1,0:T(8,128)S(1)} copy-done((f32[2,64,128]{2,1,0:T(8,128)S(1)}, f32[2,64,128]{2,1,0:T(8,128)}, u32[]{:S(2)}) %copy-start.1) | copy-done | bytes 65560
  2.4 0.0 copy-start.2
  2.4 0.8 %copy-done.2 = f32[2,64,64]{2,1,0:T(8,128)S(1)} copy-done((f32[2,64,64]{2,1,0:T(8,128)S(1)}, f32[2,64,64]{2,1,0:T(8,128)}, u32[]{:S(2)}) %copy-start.2) | copy-done | bytes 32792
  3.3 0.0 copy-start.3
  3.3 0.8 copy-done.3
  4.0 0.0 copy-start.4
  4.0 0.7 copy-done.4
  4.7 0.0 copy-start.5
  4.7 0.7 copy-done.5
  5.4 71.7 %panel.1 = (f32[2,32,64]{2,1,0:T(8,128)S(1)}, f32[2,32,1024]{2,1,0:T(8,128)S(1)}, f32[4]{0:T(128)S(1)}) custom-call(f32[2,64,128]{2,1,0:T(8,128)S(1)} %copy-done.1, f32[2,64,64]{2,1,0:T(8,128)S(1)} %copy-done.2, f32[2,32,64]{2,1,0:T(8,128)S(1)} %copy-done.3, f32[2,64,16384]{2,1,0:T(8,128)} %trail_hbm.1, f32[2,32,1024]{2,1,0:T(8,128)S(1)} %copy-done, ...), custom_call_target="tpu_custom_call" | custom-call | tf_op jit(solution)/shard_map/panel/pallas_call | solution.py:329
  77.0 0.6 copy.13
  77.6 0.7 copy.14
  78.3 0.5 copy.15
Async XLA Ops:
  0.6 1.0 %copy-start = (f32[2,32,1024]{2,1,0:T(8,128)S(1)}, f32[2,32,1024]{2,1,0:T(8,128)}, u32[]{:S(2)}) copy-start(f32[2,32,1024]{2,1,0:T(8,128)} %trail_rhs_hbm.1) | copy-start | bytes 786436
  1.6 0.8 %copy-start.1 = (f32[2,64,128]{2,1,0:T(8,128)S(1)}, f32[2,64,128]{2,1,0:T(8,128)}, u32[]{:S(2)}) copy-start(f32[2,64,128]{2,1,0:T(8,128)} %upper_ref.1) | copy-start | bytes 196612
  2.4 0.8 %copy-start.2 = (f32[2,64,64]{2,1,0:T(8,128)S(1)}, f32[2,64,64]{2,1,0:T(8,128)}, u32[]{:S(2)}) copy-start(f32[2,64,64]{2,1,0:T(8,128)} %inverse_ref.1) | copy-start | bytes 98308
  3.3 0.8 copy-start.3
  4.0 0.7 copy-start.4
  4.7 0.7 copy-start.5

commit v2 on v1

v2 whole, which is shorter than its diff:
```python
import jax
import jax.numpy as jnp
from jax import lax
from jax.experimental import pallas as pl
from jax.experimental.pallas import tpu as pltpu
from jax.sharding import PartitionSpec as P

MESH = pl.DeviceIdType.MESH
F32 = jnp.float32
BF16 = jnp.bfloat16
Y, X, Z = 0, 1, 2
DISTS = (1, 3, 2)
ORDER = (2, 1, 3, 0)


def halves(value):
    high = value.astype(BF16)
    low = (value - high.astype(F32)).astype(BF16)
    return high, low


def stacked(value):
    high, low = halves(value)
    return jnp.concatenate([high, low], axis=0)


def left_side(value):
    high, low = halves(value)
    both = jnp.concatenate([high, low], axis=0)
    return jnp.concatenate([both, both], axis=1)


def multiply(left, right):
    out = jnp.dot(left, right, preferred_element_type=F32)
    rows = out.shape[0] // 2
    return out[:rows] + out[rows:]


def conj_left(value):
    re, im = value[:, :64], value[:, 64:]
    turned = jnp.concatenate([im, -re], axis=1)
    return left_side(jnp.concatenate([value, turned], axis=0))


def body(
    upper_hbm, inverse_hbm, rhs_hbm, trail_hbm, trail_rhs_hbm, currents_hbm, owner_hbm,
    solved_ref, updated_ref, gradient_ref,
    upper_ref, inverse_ref, rhs_ref, currents_ref, owner_ref, pieces, rhs_all, held, answers, weights, trail, trail_rhs,
    first_out, first_in, second_out, second_in, third_out, third_in, fourth_in, tiles,
    local_sem, r_send, r_recv, *pairs,
):
    (y_sems, x_sems, z_sems, rhs_sems, k_sems, chain_sems, tile_sems) = zip(
        pairs[::2], pairs[1::2]
    )
    row, col = lax.axis_index("row"), lax.axis_index("col")
    me = (row // 4, row % 4, col // 2)
    core = col % 2

    def shifted(coords, dim, dist):
        moved = list(coords)
        moved[dim] = (moved[dim] + dist) % 4
        return tuple(moved)

    def device(coords, which):
        return (coords[0] * 4 + coords[1], coords[2] * 2 + which)

    def peer(dim, dist):
        if dim is None:
            return device(me, 1 - core)
        return device(shifted(me, dim, dist), core)

    early = []
    for n, (src, dst) in enumerate((
        (upper_hbm, upper_ref), (inverse_hbm, inverse_ref), (rhs_hbm, rhs_ref), (currents_hbm, currents_ref), (owner_hbm, owner_ref)
    )):
        early.append(pltpu.make_async_copy(src, dst, local_sem.at[5 + n]))
        early[n].start()
    loads = []
    for part in range(4):
        cols = pl.ds(part * 4096, 4096)
        loads.append(pltpu.make_async_copy(trail_hbm.at[:, :, cols], trail.at[:, :, cols], local_sem.at[part]))
    loads.append(pltpu.make_async_copy(trail_rhs_hbm, trail_rhs, local_sem.at[4]))
    for load in loads:
        load.start()

    barrier = pltpu.get_barrier_semaphore()
    for dim in (Y, X, Z):
        for dist in DISTS:
            pl.semaphore_signal(barrier, inc=1, device_id=peer(dim, dist), device_id_type=MESH)
    pl.semaphore_signal(barrier, inc=1, device_id=peer(None, 0), device_id_type=MESH)
    for dist in DISTS:
        there = shifted(shifted(me, Y, dist), Z, dist)
        pl.semaphore_signal(barrier, inc=1, device_id=device(there, core), device_id_type=MESH)

    for load in early:
        load.wait()

    upper = upper_ref[...].reshape(128, 128)
    inv_re, inv_im = inverse_ref[0], inverse_ref[1]
    left = jnp.concatenate(
        [jnp.concatenate([inv_re, -inv_im], axis=1), jnp.concatenate([inv_im, inv_re], axis=1)], axis=0
    )
    pieces[me[0], me[1], core] = multiply(left_side(left), stacked(upper))
    rhs_all[me[1]] = jnp.concatenate([rhs_ref[0], rhs_ref[1]], axis=1)

    pl.semaphore_wait(barrier, 13)

    y, x, z = me

    def turn(at, dist):
        moved = at + dist
        return jnp.where(moved >= 4, moved - 4, moved)

    FULL = (0,) + DISTS
    from_y = [turn(y, (4 - d) % 4) for d in FULL]
    from_x = [turn(x, (4 - d) % 4) for d in FULL]
    to_y = [turn(y, d) for d in FULL]
    to_x = [turn(x, d) for d in FULL]
    to_z = [turn(z, d) for d in FULL]
    peers = {
        Y: [(v * 4 + x, col) for v in to_y],
        X: [(y * 4 + v, col) for v in to_x],
        Z: [(row, v * 2 + core) for v in to_z],
        None: [(row, col + 1 - 2 * core)] * 4,
        "YZ": [(v * 4 + x, w * 2 + core) for v, w in zip(to_y, to_z)],
    }
    solver = y == z
    three = range(3)

    def both(first, second):
        return jnp.logical_and(first, second)

    def remote(ref, dim, i, sems, index, there=None):
        return pltpu.make_async_remote_copy(
            src_ref=ref, dst_ref=ref, send_sem=sems[0].at[index], recv_sem=sems[1].at[index if there is None else there],
            device_id=peers[dim][i + 1], device_id_type=MESH,
        )

    def run(what, cond, ref, dim, i, sems, index, there=None):
        pl.when(cond)(lambda: getattr(remote(ref(), dim, i, sems, index, there), what)())

    def needed(py, px, which):
        return jnp.logical_or(py < y, both(py == y, (px + 1) // 2 <= which))

    def go_y(what, i):
        if what == "wait_recv":
            py, cond = from_y[i + 1], both(solver, from_y[i + 1] < y)
        else:
            py, cond = y, both(y < z, to_y[i + 1] == z)
        run(what, cond, lambda: pieces.at[py, x, core], Y, i, y_sems, i)

    def go_x(what, py, i):
        px = from_x[i + 1] if what == "wait_recv" else x
        run(what, both(both(solver, py <= y), needed(py, px, core)), lambda: pieces.at[py, px, core], X, i, x_sems, (py, i))

    def go_r(what, i):
        px = from_x[i + 1] if what == "wait_recv" else x
        run(what, solver, lambda: rhs_all.at[px], X, i, rhs_sems, i)

    def go_k(what, py, px):
        which = 1 - core if what == "wait_recv" else core
        run(what, both(both(solver, py <= y), needed(py, px, which)), lambda: pieces.at[py, px, which], None, 0, k_sems, (py, px))

    def go_chain(what, i):
        if what == "wait_recv":
            at, cond = from_y[i + 1], both(solver, from_y[i + 1] < y)
        else:
            at, cond = y, both(solver, y < to_y[i + 1])
        run(what, cond, lambda: answers.at[at], "YZ", i, chain_sems, i, i)

    def go_z(what, i):
        cond = turn(z, 4 - DISTS[i]) == y if what == "wait_recv" else solver
        run(what, cond, lambda: answers.at[y, x], Z, i, z_sems, i)

    for i in three:
        go_y("start", i)
    for i in three:
        go_r("start", i)
        go_x("start", y, i)
    go_k("start", y, x)
    for i in three:
        go_y("wait_recv", i)
        for j in three:
            pl.when(from_y[i + 1] < y)(lambda i=i, j=j: go_x("start", from_y[i + 1], j))
        pl.when(from_y[i + 1] < y)(lambda i=i: go_k("start", from_y[i + 1], x))

    def upto(count, action):
        def step(index, carry):
            action(index)
            return carry
        lax.fori_loop(0, count, step, 0)

    lanes = lax.broadcasted_iota(jnp.int32, (32, 128), 1)

    @pl.when(solver)
    def _():
        def collect(py):
            for i in three:
                go_x("wait_recv", py, i)
                go_k("start", py, from_x[i + 1])

        upto(y + 1, collect)
        for i in three:
            go_r("wait_recv", i)

        def split(py):
            for px in range(4):
                go_k("wait_recv", py, px)
            for px in range(4):
                for which in range(2):
                    weights[py, px, :, which * 128:(which + 1) * 128] = stacked(pieces[py, px, which])

        upto(y + 1, split)
        held[...] = jnp.zeros_like(held)

        def earlier(at):
            for i in three:
                pl.when(from_y[i + 1] == at)(lambda i=i: go_chain("wait_recv", i))
            total = held[...]
            for px in range(4):
                total = total + multiply(conj_left(answers[at, px]), weights[at, px])
            held[...] = total

        upto(y, earlier)
        for n in range(4):
            tile = held[:, (n // 2) * 128:(n // 2 + 1) * 128]
            if n % 2 == 0:
                local = jnp.where(lanes < 64, tile[:32], pltpu.roll(tile[32:], 64, 1))
            else:
                local = jnp.where(lanes < 64, pltpu.roll(tile[:32], 64, 1), tile[32:])
            answer = rhs_all[n] - local
            answers[y, n] = answer
            first = (n + 1) // 2 * 128
            if first < 256:
                held[:, first:] += multiply(conj_left(answer), weights[y, n, :, first:])

    for i in three:
        go_chain("start", i)
    for i in three:
        go_z("start", i)
    for i in three:
        go_z("wait_recv", i)

    value = multiply(conj_left(answers[y, x]), stacked(inverse_ref[...].reshape(128, 64)))
    solved_ref[...] = value.reshape(2, 32, 64)
    lhs = conj_left(jnp.concatenate([value[:32], value[32:]], axis=1))

    total_re = jnp.sum(value[:32], axis=0, keepdims=True)
    total_im = jnp.sum(value[32:], axis=0, keepdims=True)
    partial_value = currents_ref[0:1, :] * total_re - currents_ref[1:2, :] * total_im
    tiles[me[0], me[1], 0:1, 0:64] = partial_value
    tiles[me[0], me[1], 1:2, 0:64] = owner_ref[...].astype(F32)
    tiles[me[0], me[1], 0:2, 64:128] = jnp.full((2, 64), -1.0, F32)
    tiles[me[0], me[1], 2:8, :] = jnp.zeros((6, 128), F32)
    def go_t(what, n, i):
        recv = what == "wait_recv"
        if n == 0:
            ref = tiles.at[y, from_x[i + 1] if recv else x]
        else:
            ref = tiles.at[from_y[i + 1] if recv else y]
        getattr(remote(ref, X if n == 0 else Y, i, tile_sems, (n, i)), what)()

    for i in three:
        go_t("start", 0, i)

    for load in loads:
        load.wait()

    def term(half, a, j):
        dims = (X, Y) if half == 0 else (Y, X)
        there = shifted(shifted(me, dims[0], a), dims[1], j)
        begin = pl.multiple_of((there[0] * 4 + there[1]) * 1024 + half * 512, 512)
        block = trail[:, :, pl.ds(begin, 512)].reshape(128, 512)
        return multiply(lhs, stacked(block))

    def send(src, dst, dim, dist, slot):
        copy = pltpu.make_async_remote_copy(
            src_ref=src, dst_ref=dst, send_sem=r_send.at[slot], recv_sem=r_recv.at[slot],
            device_id=peer(dim, dist), device_id_type=MESH,
        )
        copy.start()
        return copy

    DIM = ((X, Y), (Y, X))
    top, low = pl.ds(0, 32), pl.ds(32, 32)
    one, two, third, fourth = {}, {}, {}, {}
    for n, j in enumerate(ORDER):
        for h in range(2):
            first_out[h, n] = term(h, 2, j)
            slot = (h * 4 + n) * 2
            one[h, n, 0] = send(first_out.at[h, n, top], first_in.at[h, n, 0], DIM[h][0], 1, slot)
            one[h, n, 1] = send(first_out.at[h, n, low], first_in.at[h, n, 1], DIM[h][0], 3, slot + 1)
        if n == 0:
            for i in three:
                go_t("wait_recv", 0, i)
            for i in three:
                go_t("start", 1, i)
    for n, j in enumerate(ORDER):
        for h in range(2):
            slot = 16 + (h * 4 + n) * 2
            for s, a in enumerate((1, 3)):
                second_out[h, n, s] = term(h, a, j)
                one[h, n, s].wait_recv()
                rows = top if s == 0 else low
                second_out[h, n, s, rows] += first_in[h, n, s]
                two[h, n, s] = send(second_out.at[h, n, s], second_in.at[h, n, s], DIM[h][0], a, slot + s)
    for n, j in enumerate(ORDER):
        for h in range(2):
            third_out[h, n] = term(h, 0, j)
            for s in range(2):
                two[h, n, s].wait_recv()
            third_out[h, n] += second_in[h, n, 0] + second_in[h, n, 1]
            if j == 2:
                third[h, 0] = send(third_out.at[h, n, top], third_in.at[h, 0], DIM[h][1], 1, 32 + h * 4)
                third[h, 1] = send(third_out.at[h, n, low], third_in.at[h, 1], DIM[h][1], 3, 33 + h * 4)
            elif j == 0:
                for s in range(2):
                    fourth[h, s].wait_recv()
                total = third_out[h, n] + fourth_in[h, 0] + fourth_in[h, 1]
                cols = pl.ds(h * 512, 512)
                updated_ref[:, :, cols] = trail_rhs[:, :, cols] - total.reshape(2, 32, 512)
            else:
                s = 0 if j == 1 else 1
                rows = top if s == 0 else low
                third[h, s].wait_recv()
                third_out[h, n, rows] += third_in[h, s]
                fourth[h, s] = send(third_out.at[h, n], fourth_in.at[h, s], DIM[h][1], j, 34 + h * 4 + s)

    for i in three:
        go_t("wait_recv", 1, i)
    parts = tiles[...].reshape(16, 8, 128)
    for n in range(4):
        patch = ((row * 8 + col) * 4 + n).astype(F32)
        chosen = jnp.where(parts[:, 1, :] == patch, parts[:, 0, :], 0.0)
        gradient_ref[n] = jnp.sum(chosen)

    for i in three:
        go_y("wait_send", i)
        go_r("wait_send", i)
        go_chain("wait_send", i)
        go_z("wait_send", i)
        for n in range(2):
            go_t("wait_send", n, i)
    for py in range(4):
        for i in three:
            go_x("wait_send", py, i)
        for px in range(4):
            go_k("wait_send", py, px)
    for group in (one, two, third, fourth):
        for copy in group.values():
            copy.wait_send()


def on_device(upper_block, block_inverse, panel_rhs, upper_trail, trail_rhs, currents, owner):
    vmem = pl.BlockSpec(memory_space=pltpu.VMEM)
    hbm = pl.BlockSpec(memory_space=pltpu.HBM)
    dma = pltpu.SemaphoreType.DMA
    return pl.pallas_call(
        body,
        out_shape=(
            jax.ShapeDtypeStruct((2, 32, 64), F32),
            jax.ShapeDtypeStruct((2, 32, 1024), F32),
            jax.ShapeDtypeStruct((4,), F32),
        ),
        in_specs=[hbm] * 7,
        out_specs=(vmem, vmem, pl.BlockSpec(memory_space=pltpu.SMEM)),
        scratch_shapes=[
            pltpu.VMEM((2, 64, 128), F32),
            pltpu.VMEM((2, 64, 64), F32),
            pltpu.VMEM((2, 32, 64), F32),
            pltpu.VMEM((2, 64), F32),
            pltpu.VMEM((1, 64), jnp.int32),
            pltpu.VMEM((4, 4, 2, 128, 128), F32),
            pltpu.VMEM((4, 32, 128), F32),
            pltpu.VMEM((64, 256), F32),
            pltpu.VMEM((4, 4, 32, 128), F32),
            pltpu.VMEM((4, 4, 256, 256), BF16),
            pltpu.VMEM((2, 64, 16384), F32),
            pltpu.VMEM((2, 32, 1024), F32),
            pltpu.VMEM((2, 4, 64, 512), F32),
            pltpu.VMEM((2, 4, 2, 32, 512), F32),
            pltpu.VMEM((2, 4, 2, 64, 512), F32),
            pltpu.VMEM((2, 4, 2, 64, 512), F32),
            pltpu.VMEM((2, 4, 64, 512), F32),
            pltpu.VMEM((2, 2, 32, 512), F32),
            pltpu.VMEM((2, 2, 64, 512), F32),
            pltpu.VMEM((4, 4, 8, 128), F32),
            dma((10,)),
            dma((40,)), dma((40,)),
            *(
                dma(shape)
                for shape in (
                    (3,), (4, 3), (3,), (3,), (4, 4), (3,), (2, 3)
                )
                for _ in range(2)
            ),
        ],
        compiler_params=pltpu.CompilerParams(
            collective_id=0, has_side_effects=True, vmem_limit_bytes=63 * 2**20
        ),
        name="panel",
    )(upper_block, block_inverse, panel_rhs, upper_trail, trail_rhs, currents, owner.reshape(1, 64))


def solution(mesh):
    return jax.shard_map(
        on_device,
        mesh=mesh,
        in_specs=(
            P(None, "row", "col"),
            P(None, "row", None),
            P(None, None, "row"),
            P(None, "row", "col"),
            P(None, None, ("col", "row")),
            P(None, "row"),
            P("row"),
        ),
        out_specs=(P(None, None, "row"), P(None, None, ("col", "row")), P(("row", "col"))),
        check_vma=False,
    )
```

time: 80.1 us -> 67.8 us (0.85); the launches traced: 78.9 us -> 67.6 us
  Pallas kernels: 71.7 us -> 62.7 us
  local copies, waits for them, and re-layouts: 6.54 us -> 4.23 us
    pallas_call x1, Pallas kernels: 71.7 us -> 62.7 us  [on_device(): pl.pallas_call(body, out_shape=(jax.ShapeDtypeStruct((2, 32, 64), F32), j...]
    unnamed x15 -> x3, local copies, waits for them, and re-layouts: 6.54 us -> 4.23 us
where the time goes in v2:
time: 67.8 us; the launch traced here: 67.6 us
  Pallas kernels  62.7 us (92%)
  local copies, waits for them, and re-layouts  4.23 us (6%)
    pallas_call x1, Pallas kernels, on_device(): pl.pallas_call(body, out_shape=(jax.ShapeDtypeStruct((2, 32, 64), F32), j...  62.7 us
    unnamed x3, local copies, waits for them, and re-layouts  4.23 us

profile of v2, /device:TPU:0, one launch (start us, length us, event | category | flops | bytes accessed | tf_op | source)
XLA Modules:
  0.0 67.6 jit_solution(17484330506261146327)
XLA Ops:
  0.6 62.7 %panel.1 = (f32[2,32,64]{2,1,0:T(8,128)}, f32[2,32,1024]{2,1,0:T(8,128)}, f32[4]{0:T(128)}) custom-call(f32[2,64,128]{2,1,0:T(8,128)} %upper_hbm.1, f32[2,64,64]{2,1,0:T(8,128)} %inverse_hbm.1, f32[2,32,64]{2,1,0:T(8,128)} %rhs_hbm.1, f32[2,64,16384]{2,1,0:T(8,128)} %trail_hbm.1, f32[2,32,1024]{2,1,0:T(8,128)} %trail_rhs_hbm.1, f32[2,64]{1,0:T(2,128)} %currents_hbm.1, ...), custom_call_target="tpu_custom_call" | custom-call | tf_op jit(solution)/shard_map/panel/pallas_call | solution.py:358
  63.4 1.4 %copy.13 = f32[2,32,64]{2,1,0:T(8,128)} copy(f32[2,32,64]{2,1,0:T(8,128)} %get-tuple-element.6) | data formatting | bytes 32768
  64.8 1.7 %copy.14 = f32[2,32,1024]{2,1,0:T(8,128)} copy(f32[2,32,1024]{2,1,0:T(8,128)} %get-tuple-element.7) | data formatting | bytes 524288
  66.4 1.2 %copy.15 = f32[4]{0:T(128)} copy(f32[4]{0:T(128)} %get-tuple-element.8) | data formatting | bytes 32

commit v3 on v2

--- a/solution.py
+++ b/solution.py
@@ -161,12 +161,12 @@
         which = 1 - core if what == "wait_recv" else core
         run(what, both(both(solver, py <= y), needed(py, px, which)), lambda: pieces.at[py, px, which], None, 0, k_sems, (py, px))
 
-    def go_chain(what, i):
+    def go_chain(what, i, n):
         if what == "wait_recv":
             at, cond = from_y[i + 1], both(solver, from_y[i + 1] < y)
         else:
             at, cond = y, both(solver, y < to_y[i + 1])
-        run(what, cond, lambda: answers.at[at], "YZ", i, chain_sems, i, i)
+        run(what, cond, lambda: answers.at[at, n], "YZ", i, chain_sems, (i, n))
 
     def go_z(what, i):
         cond = turn(z, 4 - DISTS[i]) == y if what == "wait_recv" else solver
@@ -214,12 +214,10 @@
         held[...] = jnp.zeros_like(held)
 
         def earlier(at):
-            for i in three:
-                pl.when(from_y[i + 1] == at)(lambda i=i: go_chain("wait_recv", i))
-            total = held[...]
             for px in range(4):
-                total = total + multiply(conj_left(answers[at, px]), weights[at, px])
-            held[...] = total
+                for i in three:
+                    pl.when(from_y[i + 1] == at)(lambda i=i: go_chain("wait_recv", i, px))
+                held[...] += multiply(conj_left(answers[at, px]), weights[at, px])
 
         upto(y, earlier)
         for n in range(4):
@@ -230,14 +228,18 @@
                 local = jnp.where(lanes < 64, pltpu.roll(tile[:32], 64, 1), tile[32:])
             answer = rhs_all[n] - local
             answers[y, n] = answer
+            for i in three:
+                pl.when(y < to_y[i + 1])(lambda i=i: go_chain("start", i, n))
+
+            @pl.when(x == n)
+            def _():
+                for i in three:
+                    go_z("start", i)
+
             first = (n + 1) // 2 * 128
             if first < 256:
                 held[:, first:] += multiply(conj_left(answer), weights[y, n, :, first:])
 
-    for i in three:
-        go_chain("start", i)
-    for i in three:
-        go_z("start", i)
     for i in three:
         go_z("wait_recv", i)
 
@@ -295,18 +297,21 @@
                 go_t("wait_recv", 0, i)
             for i in three:
                 go_t("start", 1, i)
-    for n, j in enumerate(ORDER):
+    def pass_on(n):
         for h in range(2):
             slot = 16 + (h * 4 + n) * 2
             for s, a in enumerate((1, 3)):
-                second_out[h, n, s] = term(h, a, j)
+                second_out[h, n, s] = term(h, a, ORDER[n])
                 one[h, n, s].wait_recv()
                 rows = top if s == 0 else low
                 second_out[h, n, s, rows] += first_in[h, n, s]
                 two[h, n, s] = send(second_out.at[h, n, s], second_in.at[h, n, s], DIM[h][0], a, slot + s)
-    for n, j in enumerate(ORDER):
+
+    def finish(n):
+        j = ORDER[n]
         for h in range(2):
             third_out[h, n] = term(h, 0, j)
+        for h in range(2):
             for s in range(2):
                 two[h, n, s].wait_recv()
             third_out[h, n] += second_in[h, n, 0] + second_in[h, n, 1]
@@ -326,18 +331,31 @@
                 third_out[h, n, rows] += third_in[h, s]
                 fourth[h, s] = send(third_out.at[h, n], fourth_in.at[h, s], DIM[h][1], j, 34 + h * 4 + s)
 
+    pass_on(0)
+    pass_on(1)
+    finish(0)
+    pass_on(2)
+    finish(1)
+    pass_on(3)
+    finish(2)
+    finish(3)
+
     for i in three:
         go_t("wait_recv", 1, i)
     parts = tiles[...].reshape(16, 8, 128)
+    places = lax.broadcasted_iota(jnp.int32, (1, 128), 1)
+    sums = jnp.zeros((1, 128), F32)
     for n in range(4):
         patch = ((row * 8 + col) * 4 + n).astype(F32)
         chosen = jnp.where(parts[:, 1, :] == patch, parts[:, 0, :], 0.0)
-        gradient_ref[n] = jnp.sum(chosen)
+        sums = jnp.where(places == n, jnp.sum(chosen, keepdims=True), sums)
+    gradient_ref[...] = sums[:, :4]
 
     for i in three:
         go_y("wait_send", i)
         go_r("wait_send", i)
-        go_chain("wait_send", i)
+        for n in range(4):
+            go_chain("wait_send", i, n)
         go_z("wait_send", i)
         for n in range(2):
             go_t("wait_send", n, i)
@@ -355,15 +373,15 @@
     vmem = pl.BlockSpec(memory_space=pltpu.VMEM)
     hbm = pl.BlockSpec(memory_space=pltpu.HBM)
     dma = pltpu.SemaphoreType.DMA
-    return pl.pallas_call(
+    solved, updated, gradient = pl.pallas_call(
         body,
         out_shape=(
-            jax.ShapeDtypeStruct((2, 32, 64), F32),
-            jax.ShapeDtypeStruct((2, 32, 1024), F32),
-            jax.ShapeDtypeStruct((4,), F32),
+            pltpu.VMEM((2, 32, 64), F32),
+            pltpu.VMEM((2, 32, 1024), F32),
+            pltpu.VMEM((1, 4), F32),
         ),
         in_specs=[hbm] * 7,
-        out_specs=(vmem, vmem, pl.BlockSpec(memory_space=pltpu.SMEM)),
+        out_specs=(vmem, vmem, vmem),
         scratch_shapes=[
             pltpu.VMEM((2, 64, 128), F32),
             pltpu.VMEM((2, 64, 64), F32),
@@ -390,7 +408,7 @@
             *(
                 dma(shape)
                 for shape in (
-                    (3,), (4, 3), (3,), (3,), (4, 4), (3,), (2, 3)
+                    (3,), (4, 3), (3,), (3,), (4, 4), (3, 4), (2, 3)
                 )
                 for _ in range(2)
             ),
@@ -400,6 +418,7 @@
         ),
         name="panel",
     )(upper_block, block_inverse, panel_rhs, upper_trail, trail_rhs, currents, owner.reshape(1, 64))
+    return solved, updated, gradient.reshape(4)
 
 
 def solution(mesh):

time: 67.8 us -> 60.7 us (0.90)
  Pallas kernels: 62.7 us -> 58.2 us
  local copies, waits for them, and re-layouts: 4.23 us -> 1.83 us
    pallas_call x1, Pallas kernels: 62.7 us -> 58.2 us  [on_device(): pl.pallas_call(body, out_shape=(pltpu.VMEM((2, 32, 64), F32), pltpu.VMEM(...]
    unnamed x3, local copies, waits for them, and re-layouts: 4.23 us -> 1.83 us
where the time goes in v3:
time: 60.7 us; the launch traced here: 60.6 us
  Pallas kernels  58.2 us (96%)
  local copies, waits for them, and re-layouts  1.83 us (3%)
  between operations  0.64 us (1%)
    pallas_call x1, Pallas kernels, on_device(): pl.pallas_call(body, out_shape=(pltpu.VMEM((2, 32, 64), F32), pltpu.VMEM(...  58.2 us
    unnamed x3, local copies, waits for them, and re-layouts  1.83 us

profile of v3, /device:TPU:0, one launch (start us, length us, event | category | flops | bytes accessed | tf_op | source)
XLA Modules:
  0.0 60.6 jit_solution(14498644507956940366)
XLA Ops:
  0.6 58.2 %panel.1 = (f32[2,32,64]{2,1,0:T(8,128)S(1)}, f32[2,32,1024]{2,1,0:T(8,128)S(1)}, f32[1,4]{1,0:T(1,128)S(1)}) custom-call(f32[2,64,128]{2,1,0:T(8,128)} %upper_hbm.1, f32[2,64,64]{2,1,0:T(8,128)} %inverse_hbm.1, f32[2,32,64]{2,1,0:T(8,128)} %rhs_hbm.1, f32[2,64,16384]{2,1,0:T(8,128)} %trail_hbm.1, f32[2,32,1024]{2,1,0:T(8,128)} %trail_rhs_hbm.1, ...), custom_call_target="tpu_custom_call" | custom-call | tf_op jit(solution)/shard_map/panel/pallas_call | solution.py:376
  58.8 0.6 %copy.13 = f32[2,32,64]{2,1,0:T(8,128)} copy(f32[2,32,64]{2,1,0:T(8,128)S(1)} %get-tuple-element.9) | data formatting | bytes 32768
  59.4 0.5 copy.15
  59.9 0.7 %copy.14 = f32[2,32,1024]{2,1,0:T(8,128)} copy(f32[2,32,1024]{2,1,0:T(8,128)S(1)} %get-tuple-element.10) | data formatting | bytes 524288

commit v4 on v3

--- a/solution.py
+++ b/solution.py
@@ -11,6 +11,9 @@
 Y, X, Z = 0, 1, 2
 DISTS = (1, 3, 2)
 ORDER = (2, 1, 3, 0)
+CUT, LAG = 1, 2
+UNITS = tuple((j, c) for j in ORDER for c in range(CUT))
+WIDE = 512 // CUT
 
 
 def halves(value):
@@ -175,9 +178,10 @@
     for i in three:
         go_y("start", i)
     for i in three:
-        go_r("start", i)
         go_x("start", y, i)
     go_k("start", y, x)
+    for i in three:
+        go_r("start", i)
     for i in three:
         go_y("wait_recv", i)
         for j in three:
@@ -268,11 +272,12 @@
     for load in loads:
         load.wait()
 
-    def term(half, a, j):
+    def term(half, a, unit):
+        j, c = UNITS[unit]
         dims = (X, Y) if half == 0 else (Y, X)
         there = shifted(shifted(me, dims[0], a), dims[1], j)
-        begin = pl.multiple_of((there[0] * 4 + there[1]) * 1024 + half * 512, 512)
-        block = trail[:, :, pl.ds(begin, 512)].reshape(128, 512)
+        begin = pl.multiple_of((there[0] * 4 + there[1]) * 1024 + (half * 512 + c * WIDE), WIDE)
+        block = trail[:, :, pl.ds(begin, WIDE)].reshape(128, WIDE)
         return multiply(lhs, stacked(block))
 
     def send(src, dst, dim, dist, slot):
@@ -286,59 +291,59 @@
     DIM = ((X, Y), (Y, X))
     top, low = pl.ds(0, 32), pl.ds(32, 32)
     one, two, third, fourth = {}, {}, {}, {}
-    for n, j in enumerate(ORDER):
+    count = len(UNITS)
+    for n in range(count):
         for h in range(2):
-            first_out[h, n] = term(h, 2, j)
-            slot = (h * 4 + n) * 2
+            first_out[h, n] = term(h, 2, n)
+            slot = (h * count + n) * 2
             one[h, n, 0] = send(first_out.at[h, n, top], first_in.at[h, n, 0], DIM[h][0], 1, slot)
             one[h, n, 1] = send(first_out.at[h, n, low], first_in.at[h, n, 1], DIM[h][0], 3, slot + 1)
-        if n == 0:
+
+    def pass_on(n):
+        for h in range(2):
+            slot = (2 * count + h * count + n) * 2
+            for s, a in enumerate((1, 3)):
+                second_out[h, n, s] = term(h, a, n)
+                one[h, n, s].wait_recv()
+                rows = top if s == 0 else low
+                second_out[h, n, s, rows] += first_in[h, n, s]
+                two[h, n, s] = send(second_out.at[h, n, s], second_in.at[h, n, s], DIM[h][0], a, slot + s)
+
+    def finish(n):
+        j, c = UNITS[n]
+        for h in range(2):
+            third_out[h, n] = term(h, 0, n)
+        for h in range(2):
+            slot = 8 * count + (h * CUT + c) * 4
+            for s in range(2):
+                two[h, n, s].wait_recv()
+            third_out[h, n] += second_in[h, n, 0] + second_in[h, n, 1]
+            if j == 2:
+                third[h, c, 0] = send(third_out.at[h, n, top], third_in.at[h, c, 0], DIM[h][1], 1, slot)
+                third[h, c, 1] = send(third_out.at[h, n, low], third_in.at[h, c, 1], DIM[h][1], 3, slot + 1)
+            elif j == 0:
+                for s in range(2):
+                    fourth[h, c, s].wait_recv()
+                total = third_out[h, n] + fourth_in[h, c, 0] + fourth_in[h, c, 1]
+                cols = pl.ds(h * 512 + c * WIDE, WIDE)
+                updated_ref[:, :, cols] = trail_rhs[:, :, cols] - total.reshape(2, 32, WIDE)
+            else:
+                s = 0 if j == 1 else 1
+                rows = top if s == 0 else low
+                third[h, c, s].wait_recv()
+                third_out[h, n, rows] += third_in[h, c, s]
+                fourth[h, c, s] = send(third_out.at[h, n], fourth_in.at[h, c, s], DIM[h][1], j, slot + 2 + s)
+
+    for n in range(count + LAG):
+        if n >= LAG:
+            finish(n - LAG)
+        if n < count:
+            pass_on(n)
+        if n == LAG:
             for i in three:
                 go_t("wait_recv", 0, i)
             for i in three:
                 go_t("start", 1, i)
-    def pass_on(n):
-        for h in range(2):
-            slot = 16 + (h * 4 + n) * 2
-            for s, a in enumerate((1, 3)):
-                second_out[h, n, s] = term(h, a, ORDER[n])
-                one[h, n, s].wait_recv()
-                rows = top if s == 0 else low
-                second_out[h, n, s, rows] += first_in[h, n, s]
-                two[h, n, s] = send(second_out.at[h, n, s], second_in.at[h, n, s], DIM[h][0], a, slot + s)
-
-    def finish(n):
-        j = ORDER[n]
-        for h in range(2):
-            third_out[h, n] = term(h, 0, j)
-        for h in range(2):
-            for s in range(2):
-                two[h, n, s].wait_recv()
-            third_out[h, n] += second_in[h, n, 0] + second_in[h, n, 1]
-            if j == 2:
-                third[h, 0] = send(third_out.at[h, n, top], third_in.at[h, 0], DIM[h][1], 1, 32 + h * 4)
-                third[h, 1] = send(third_out.at[h, n, low], third_in.at[h, 1], DIM[h][1], 3, 33 + h * 4)
-            elif j == 0:
-                for s in range(2):
-                    fourth[h, s].wait_recv()
-                total = third_out[h, n] + fourth_in[h, 0] + fourth_in[h, 1]
-                cols = pl.ds(h * 512, 512)
-                updated_ref[:, :, cols] = trail_rhs[:, :, cols] - total.reshape(2, 32, 512)
-            else:
-                s = 0 if j == 1 else 1
-                rows = top if s == 0 else low
-                third[h, s].wait_recv()
-                third_out[h, n, rows] += third_in[h, s]
-                fourth[h, s] = send(third_out.at[h, n], fourth_in.at[h, s], DIM[h][1], j, 34 + h * 4 + s)
-
-    pass_on(0)
-    pass_on(1)
-    finish(0)
-    pass_on(2)
-    finish(1)
-    pass_on(3)
-    finish(2)
-    finish(3)
 
     for i in three:
         go_t("wait_recv", 1, i)
@@ -395,16 +400,16 @@
             pltpu.VMEM((4, 4, 256, 256), BF16),
             pltpu.VMEM((2, 64, 16384), F32),
             pltpu.VMEM((2, 32, 1024), F32),
-            pltpu.VMEM((2, 4, 64, 512), F32),
-            pltpu.VMEM((2, 4, 2, 32, 512), F32),
-            pltpu.VMEM((2, 4, 2, 64, 512), F32),
-            pltpu.VMEM((2, 4, 2, 64, 512), F32),
-            pltpu.VMEM((2, 4, 64, 512), F32),
-            pltpu.VMEM((2, 2, 32, 512), F32),
-            pltpu.VMEM((2, 2, 64, 512), F32),
+            pltpu.VMEM((2, 4 * CUT, 64, WIDE), F32),
+            pltpu.VMEM((2, 4 * CUT, 2, 32, WIDE), F32),
+            pltpu.VMEM((2, 4 * CUT, 2, 64, WIDE), F32),
+            pltpu.VMEM((2, 4 * CUT, 2, 64, WIDE), F32),
+            pltpu.VMEM((2, 4 * CUT, 64, WIDE), F32),
+            pltpu.VMEM((2, CUT, 2, 32, WIDE), F32),
+            pltpu.VMEM((2, CUT, 2, 64, WIDE), F32),
             pltpu.VMEM((4, 4, 8, 128), F32),
             dma((10,)),
-            dma((40,)), dma((40,)),
+            dma((40 * CUT,)), dma((40 * CUT,)),
             *(
                 dma(shape)
                 for shape in (

time: 60.7 us -> 59 us (0.972)
  Pallas kernels: 58.2 us -> 56.4 us
    pallas_call x1, Pallas kernels: 58.2 us -> 56.4 us  [on_device(): pl.pallas_call(body, out_shape=(pltpu.VMEM((2, 32, 64), F32), pltpu.VMEM(...]
where the time goes in v4:
time: 59 us; the launch traced here: 58.9 us
  Pallas kernels  56.4 us (96%)
  local copies, waits for them, and re-layouts  1.83 us (3%)
  between operations  0.64 us (1%)
    pallas_call x1, Pallas kernels, on_device(): pl.pallas_call(body, out_shape=(pltpu.VMEM((2, 32, 64), F32), pltpu.VMEM(...  56.4 us
    unnamed x3, local copies, waits for them, and re-layouts  1.83 us

profile of v4, /device:TPU:0, one launch (start us, length us, event | category | flops | bytes accessed | tf_op | source)
XLA Modules:
  0.0 58.9 jit_solution(9006214368791758406)
XLA Ops:
  0.6 56.4 %panel.1 = (f32[2,32,64]{2,1,0:T(8,128)S(1)}, f32[2,32,1024]{2,1,0:T(8,128)S(1)}, f32[1,4]{1,0:T(1,128)S(1)}) custom-call(f32[2,64,128]{2,1,0:T(8,128)} %upper_hbm.1, f32[2,64,64]{2,1,0:T(8,128)} %inverse_hbm.1, f32[2,32,64]{2,1,0:T(8,128)} %rhs_hbm.1, f32[2,64,16384]{2,1,0:T(8,128)} %trail_hbm.1, f32[2,32,1024]{2,1,0:T(8,128)} %trail_rhs_hbm.1, ...), custom_call_target="tpu_custom_call" | custom-call | tf_op jit(solution)/shard_map/panel/pallas_call | solution.py:381
  57.0 0.6 %copy.13 = f32[2,32,64]{2,1,0:T(8,128)} copy(f32[2,32,64]{2,1,0:T(8,128)S(1)} %get-tuple-element.9) | data formatting | bytes 32768
  57.7 0.5 copy.15
  58.2 0.7 %copy.14 = f32[2,32,1024]{2,1,0:T(8,128)} copy(f32[2,32,1024]{2,1,0:T(8,128)S(1)} %get-tuple-element.10) | data formatting | bytes 524288

commit v5 on v4

--- a/solution.py
+++ b/solution.py
@@ -11,7 +11,8 @@
 Y, X, Z = 0, 1, 2
 DISTS = (1, 3, 2)
 ORDER = (2, 1, 3, 0)
-CUT, LAG = 1, 2
+CUT = 1
+STEPS = ("p0", "p1", "f0", "p2", "tiles", "p3", "f1", "f2", "patches", "f3")
 UNITS = tuple((j, c) for j in ORDER for c in range(CUT))
 WIDE = 512 // CUT
 
@@ -48,7 +49,7 @@
 def body(
     upper_hbm, inverse_hbm, rhs_hbm, trail_hbm, trail_rhs_hbm, currents_hbm, owner_hbm,
     solved_ref, updated_ref, gradient_ref,
-    upper_ref, inverse_ref, rhs_ref, currents_ref, owner_ref, pieces, rhs_all, held, answers, weights, trail, trail_rhs,
+    upper_ref, inverse_ref, rhs_ref, currents_ref, owner_ref, pieces, rhs_all, held, answers, weights, inverse_w, trail, trail_rhs,
     first_out, first_in, second_out, second_in, third_out, third_in, fourth_in, tiles,
     local_sem, r_send, r_recv, *pairs,
 ):
@@ -244,20 +245,27 @@
             if first < 256:
                 held[:, first:] += multiply(conj_left(answer), weights[y, n, :, first:])
 
+    for load in loads:
+        load.wait()
+    inverse_w[...] = stacked(inverse_ref[...].reshape(128, 64))
     for i in three:
         go_z("wait_recv", i)
 
-    value = multiply(conj_left(answers[y, x]), stacked(inverse_ref[...].reshape(128, 64)))
-    solved_ref[...] = value.reshape(2, 32, 64)
+    value = multiply(conj_left(answers[y, x]), inverse_w[...])
     lhs = conj_left(jnp.concatenate([value[:32], value[32:]], axis=1))
 
-    total_re = jnp.sum(value[:32], axis=0, keepdims=True)
-    total_im = jnp.sum(value[32:], axis=0, keepdims=True)
-    partial_value = currents_ref[0:1, :] * total_re - currents_ref[1:2, :] * total_im
-    tiles[me[0], me[1], 0:1, 0:64] = partial_value
-    tiles[me[0], me[1], 1:2, 0:64] = owner_ref[...].astype(F32)
-    tiles[me[0], me[1], 0:2, 64:128] = jnp.full((2, 64), -1.0, F32)
-    tiles[me[0], me[1], 2:8, :] = jnp.zeros((6, 128), F32)
+    def partials():
+        solved_ref[...] = value.reshape(2, 32, 64)
+        total_re = jnp.sum(value[:32], axis=0, keepdims=True)
+        total_im = jnp.sum(value[32:], axis=0, keepdims=True)
+        partial_value = currents_ref[0:1, :] * total_re - currents_ref[1:2, :] * total_im
+        tiles[me[0], me[1], 0:1, 0:64] = partial_value
+        tiles[me[0], me[1], 1:2, 0:64] = owner_ref[...].astype(F32)
+        tiles[me[0], me[1], 0:2, 64:128] = jnp.full((2, 64), -1.0, F32)
+        tiles[me[0], me[1], 2:8, :] = jnp.zeros((6, 128), F32)
+        for i in three:
+            go_t("start", 0, i)
+
     def go_t(what, n, i):
         recv = what == "wait_recv"
         if n == 0:
@@ -265,12 +273,6 @@
         else:
             ref = tiles.at[from_y[i + 1] if recv else y]
         getattr(remote(ref, X if n == 0 else Y, i, tile_sems, (n, i)), what)()
-
-    for i in three:
-        go_t("start", 0, i)
-
-    for load in loads:
-        load.wait()
 
     def term(half, a, unit):
         j, c = UNITS[unit]
@@ -298,6 +300,8 @@
             slot = (h * count + n) * 2
             one[h, n, 0] = send(first_out.at[h, n, top], first_in.at[h, n, 0], DIM[h][0], 1, slot)
             one[h, n, 1] = send(first_out.at[h, n, low], first_in.at[h, n, 1], DIM[h][0], 3, slot + 1)
+        if n == 1:
+            partials()
 
     def pass_on(n):
         for h in range(2):
@@ -334,41 +338,45 @@
                 third_out[h, n, rows] += third_in[h, c, s]
                 fourth[h, c, s] = send(third_out.at[h, n], fourth_in.at[h, c, s], DIM[h][1], j, slot + 2 + s)
 
-    for n in range(count + LAG):
-        if n >= LAG:
-            finish(n - LAG)
-        if n < count:
-            pass_on(n)
-        if n == LAG:
+    def gather_patches():
+        for i in three:
+            go_t("wait_recv", 1, i)
+        parts = tiles[...].reshape(16, 8, 128)
+        places = lax.broadcasted_iota(jnp.int32, (1, 128), 1)
+        sums = jnp.zeros((1, 128), F32)
+        for n in range(4):
+            patch = ((row * 8 + col) * 4 + n).astype(F32)
+            chosen = jnp.where(parts[:, 1, :] == patch, parts[:, 0, :], 0.0)
+            sums = jnp.where(places == n, jnp.sum(chosen, keepdims=True), sums)
+        gradient_ref[...] = sums[:, :4]
+
+        for i in three:
+            go_y("wait_send", i)
+            go_r("wait_send", i)
+            for n in range(4):
+                go_chain("wait_send", i, n)
+            go_z("wait_send", i)
+            for n in range(2):
+                go_t("wait_send", n, i)
+        for py in range(4):
+            for i in three:
+                go_x("wait_send", py, i)
+            for px in range(4):
+                go_k("wait_send", py, px)
+
+    for step in STEPS:
+        if step == "tiles":
             for i in three:
                 go_t("wait_recv", 0, i)
             for i in three:
                 go_t("start", 1, i)
-
-    for i in three:
-        go_t("wait_recv", 1, i)
-    parts = tiles[...].reshape(16, 8, 128)
-    places = lax.broadcasted_iota(jnp.int32, (1, 128), 1)
-    sums = jnp.zeros((1, 128), F32)
-    for n in range(4):
-        patch = ((row * 8 + col) * 4 + n).astype(F32)
-        chosen = jnp.where(parts[:, 1, :] == patch, parts[:, 0, :], 0.0)
-        sums = jnp.where(places == n, jnp.sum(chosen, keepdims=True), sums)
-    gradient_ref[...] = sums[:, :4]
-
-    for i in three:
-        go_y("wait_send", i)
-        go_r("wait_send", i)
-        for n in range(4):
-            go_chain("wait_send", i, n)
-        go_z("wait_send", i)
-        for n in range(2):
-            go_t("wait_send", n, i)
-    for py in range(4):
-        for i in three:
-            go_x("wait_send", py, i)
-        for px in range(4):
-            go_k("wait_send", py, px)
+        elif step == "patches":
+            gather_patches()
+        elif step[0] == "p":
+            pass_on(int(step[1]))
+        else:
+            finish(int(step[1]))
+
     for group in (one, two, third, fourth):
         for copy in group.values():
             copy.wait_send()
@@ -398,6 +406,7 @@
             pltpu.VMEM((64, 256), F32),
             pltpu.VMEM((4, 4, 32, 128), F32),
             pltpu.VMEM((4, 4, 256, 256), BF16),
+            pltpu.VMEM((256, 64), BF16),
             pltpu.VMEM((2, 64, 16384), F32),
             pltpu.VMEM((2, 32, 1024), F32),
             pltpu.VMEM((2, 4 * CUT, 64, WIDE), F32),

time: 59 us -> 58.5 us (level)
  no operation moved by 1% of the time
where the time goes in v5:
time: 58.5 us; the launch traced here: 58.4 us
  Pallas kernels  55.9 us (96%)
  local copies, waits for them, and re-layouts  1.83 us (3%)
  between operations  0.64 us (1%)
    pallas_call x1, Pallas kernels, on_device(): pl.pallas_call(body, out_shape=(pltpu.VMEM((2, 32, 64), F32), pltpu.VMEM(...  55.9 us
    unnamed x3, local copies, waits for them, and re-layouts  1.83 us

profile of v5, /device:TPU:0, one launch (start us, length us, event | category | flops | bytes accessed | tf_op | source)
XLA Modules:
  0.0 58.4 jit_solution(3070588207235834691)
XLA Ops:
  0.6 55.9 %panel.1 = (f32[2,32,64]{2,1,0:T(8,128)S(1)}, f32[2,32,1024]{2,1,0:T(8,128)S(1)}, f32[1,4]{1,0:T(1,128)S(1)}) custom-call(f32[2,64,128]{2,1,0:T(8,128)} %upper_hbm.1, f32[2,64,64]{2,1,0:T(8,128)} %inverse_hbm.1, f32[2,32,64]{2,1,0:T(8,128)} %rhs_hbm.1, f32[2,64,16384]{2,1,0:T(8,128)} %trail_hbm.1, f32[2,32,1024]{2,1,0:T(8,128)} %trail_rhs_hbm.1, ...), custom_call_target="tpu_custom_call" | custom-call | tf_op jit(solution)/shard_map/panel/pallas_call | solution.py:389
  56.5 0.6 %copy.13 = f32[2,32,64]{2,1,0:T(8,128)} copy(f32[2,32,64]{2,1,0:T(8,128)S(1)} %get-tuple-element.9) | data formatting | bytes 32768
  57.1 0.5 copy.15
  57.7 0.7 %copy.14 = f32[2,32,1024]{2,1,0:T(8,128)} copy(f32[2,32,1024]{2,1,0:T(8,128)S(1)} %get-tuple-element.10) | data formatting | bytes 524288

commit v6 on v5

--- a/solution.py
+++ b/solution.py
@@ -49,7 +49,7 @@
 def body(
     upper_hbm, inverse_hbm, rhs_hbm, trail_hbm, trail_rhs_hbm, currents_hbm, owner_hbm,
     solved_ref, updated_ref, gradient_ref,
-    upper_ref, inverse_ref, rhs_ref, currents_ref, owner_ref, pieces, rhs_all, held, answers, weights, inverse_w, trail, trail_rhs,
+    upper_ref, inverse_ref, rhs_ref, currents_ref, owner_ref, pieces, rhs_all, held, answers, answer_halves, weights, inverse_w, trail, trail_rhs,
     first_out, first_in, second_out, second_in, third_out, third_in, fourth_in, tiles,
     local_sem, r_send, r_recv, *pairs,
 ):
@@ -95,6 +95,7 @@
     for dist in DISTS:
         there = shifted(shifted(me, Y, dist), Z, dist)
         pl.semaphore_signal(barrier, inc=1, device_id=device(there, core), device_id_type=MESH)
+        pl.semaphore_signal(barrier, inc=1, device_id=device(shifted(me, Z, dist), 1 - core), device_id_type=MESH)
 
     for load in early:
         load.wait()
@@ -105,9 +106,10 @@
         [jnp.concatenate([inv_re, -inv_im], axis=1), jnp.concatenate([inv_im, inv_re], axis=1)], axis=0
     )
     pieces[me[0], me[1], core] = multiply(left_side(left), stacked(upper))
-    rhs_all[me[1]] = jnp.concatenate([rhs_ref[0], rhs_ref[1]], axis=1)
-
-    pl.semaphore_wait(barrier, 13)
+    mine = pl.ds(pl.multiple_of(core * 16, 16), 16)
+    rhs_all[me[1]] = jnp.concatenate([rhs_ref[0, mine], rhs_ref[1, mine]], axis=1)
+
+    pl.semaphore_wait(barrier, 16)
 
     y, x, z = me
 
@@ -137,7 +139,7 @@
     def remote(ref, dim, i, sems, index, there=None):
         return pltpu.make_async_remote_copy(
             src_ref=ref, dst_ref=ref, send_sem=sems[0].at[index], recv_sem=sems[1].at[index if there is None else there],
-            device_id=peers[dim][i + 1], device_id_type=MESH,
+            device_id=dim if isinstance(dim, tuple) else peers[dim][i + 1], device_id_type=MESH,
         )
 
     def run(what, cond, ref, dim, i, sems, index, there=None):
@@ -172,9 +174,17 @@
             at, cond = y, both(solver, y < to_y[i + 1])
         run(what, cond, lambda: answers.at[at, n], "YZ", i, chain_sems, (i, n))
 
-    def go_z(what, i):
-        cond = turn(z, 4 - DISTS[i]) == y if what == "wait_recv" else solver
-        run(what, cond, lambda: answers.at[y, x], Z, i, z_sems, i)
+    def go_z(what, i, cross):
+        recv = what == "wait_recv"
+        k = (1 - core if cross else core) if recv else core
+        if i == 3:
+            cond, there = y == z, (row, col + 1 - 2 * core)
+        else:
+            cond = turn(z, 4 - DISTS[i]) == y if recv else y == z
+            there = (row, to_z[i + 1] * 2 + (1 - core if cross else core))
+        run(what, cond, lambda: answer_halves.at[k], there, i, z_sems, (i, cross))
+
+    targets = [(i, cross) for i in three for cross in (0, 1)] + [(3, 1)]
 
     for i in three:
         go_y("start", i)
@@ -195,7 +205,7 @@
             return carry
         lax.fori_loop(0, count, step, 0)
 
-    lanes = lax.broadcasted_iota(jnp.int32, (32, 128), 1)
+    lanes = lax.broadcasted_iota(jnp.int32, (16, 128), 1)
 
     @pl.when(solver)
     def _():
@@ -228,9 +238,9 @@
         for n in range(4):
             tile = held[:, (n // 2) * 128:(n // 2 + 1) * 128]
             if n % 2 == 0:
-                local = jnp.where(lanes < 64, tile[:32], pltpu.roll(tile[32:], 64, 1))
+                local = jnp.where(lanes < 64, tile[:16], pltpu.roll(tile[16:], 64, 1))
             else:
-                local = jnp.where(lanes < 64, pltpu.roll(tile[:32], 64, 1), tile[32:])
+                local = jnp.where(lanes < 64, pltpu.roll(tile[:16], 64, 1), tile[16:])
             answer = rhs_all[n] - local
             answers[y, n] = answer
             for i in three:
@@ -238,8 +248,9 @@
 
             @pl.when(x == n)
             def _():
-                for i in three:
-                    go_z("start", i)
+                answer_halves[core] = answer
+                for i, cross in targets:
+                    go_z("start", i, cross)
 
             first = (n + 1) // 2 * 128
             if first < 256:
@@ -248,10 +259,10 @@
     for load in loads:
         load.wait()
     inverse_w[...] = stacked(inverse_ref[...].reshape(128, 64))
-    for i in three:
-        go_z("wait_recv", i)
-
-    value = multiply(conj_left(answers[y, x]), inverse_w[...])
+    for i, cross in targets:
+        go_z("wait_recv", i, cross)
+
+    value = multiply(conj_left(answer_halves[...].reshape(32, 128)), inverse_w[...])
     lhs = conj_left(jnp.concatenate([value[:32], value[32:]], axis=1))
 
     def partials():
@@ -355,7 +366,8 @@
             go_r("wait_send", i)
             for n in range(4):
                 go_chain("wait_send", i, n)
-            go_z("wait_send", i)
+            for cross in (0, 1):
+                go_z("wait_send", i, cross)
             for n in range(2):
                 go_t("wait_send", n, i)
         for py in range(4):
@@ -363,6 +375,7 @@
                 go_x("wait_send", py, i)
             for px in range(4):
                 go_k("wait_send", py, px)
+        go_z("wait_send", 3, 1)
 
     for step in STEPS:
         if step == "tiles":
@@ -402,9 +415,10 @@
             pltpu.VMEM((2, 64), F32),
             pltpu.VMEM((1, 64), jnp.int32),
             pltpu.VMEM((4, 4, 2, 128, 128), F32),
-            pltpu.VMEM((4, 32, 128), F32),
-            pltpu.VMEM((64, 256), F32),
-            pltpu.VMEM((4, 4, 32, 128), F32),
+            pltpu.VMEM((4, 16, 128), F32),
+            pltpu.VMEM((32, 256), F32),
+            pltpu.VMEM((4, 4, 16, 128), F32),
+            pltpu.VMEM((2, 16, 128), F32),
             pltpu.VMEM((4, 4, 256, 256), BF16),
             pltpu.VMEM((256, 64), BF16),
             pltpu.VMEM((2, 64, 16384), F32),
@@ -422,7 +436,7 @@
             *(
                 dma(shape)
                 for shape in (
-                    (3,), (4, 3), (3,), (3,), (4, 4), (3, 4), (2, 3)
+                    (3,), (4, 3), (4, 2), (3,), (4, 4), (3, 4), (2, 3)
                 )
                 for _ in range(2)
             ),

time: 58.5 us -> 58.3 us (level)
  no operation moved by 1% of the time
where the time goes in v6:
time: 58.3 us; the launch traced here: 58.1 us
  Pallas kernels  55.7 us (96%)
  local copies, waits for them, and re-layouts  1.83 us (3%)
  between operations  0.64 us (1%)
    pallas_call x1, Pallas kernels, on_device(): pl.pallas_call(body, out_shape=(pltpu.VMEM((2, 32, 64), F32), pltpu.VMEM(...  55.7 us
    unnamed x3, local copies, waits for them, and re-layouts  1.83 us

profile of v6, /device:TPU:0, one launch (start us, length us, event | category | flops | bytes accessed | tf_op | source)
XLA Modules:
  0.0 58.1 jit_solution(8946389048408949080)
XLA Ops:
  0.6 55.7 %panel.1 = (f32[2,32,64]{2,1,0:T(8,128)S(1)}, f32[2,32,1024]{2,1,0:T(8,128)S(1)}, f32[1,4]{1,0:T(1,128)S(1)}) custom-call(f32[2,64,128]{2,1,0:T(8,128)} %upper_hbm.1, f32[2,64,64]{2,1,0:T(8,128)} %inverse_hbm.1, f32[2,32,64]{2,1,0:T(8,128)} %rhs_hbm.1, f32[2,64,16384]{2,1,0:T(8,128)} %trail_hbm.1, f32[2,32,1024]{2,1,0:T(8,128)} %trail_rhs_hbm.1, ...), custom_call_target="tpu_custom_call" | custom-call | tf_op jit(solution)/shard_map/panel/pallas_call | solution.py:402
  56.3 0.6 %copy.13 = f32[2,32,64]{2,1,0:T(8,128)} copy(f32[2,32,64]{2,1,0:T(8,128)S(1)} %get-tuple-element.9) | data formatting | bytes 32768
  56.9 0.5 copy.15
  57.4 0.7 %copy.14 = f32[2,32,1024]{2,1,0:T(8,128)} copy(f32[2,32,1024]{2,1,0:T(8,128)S(1)} %get-tuple-element.10) | data formatting | bytes 524288

commit v7 on v6

--- a/solution.py
+++ b/solution.py
@@ -315,7 +315,7 @@
             partials()
 
     def pass_on(n):
-        for h in range(2):
+        for h in (1, 0):
             slot = (2 * count + h * count + n) * 2
             for s, a in enumerate((1, 3)):
                 second_out[h, n, s] = term(h, a, n)

time: 58.3 us -> 58.3 us (level)
  no operation moved by 1% of the time
where the time goes in v7:
time: 58.3 us; the launch traced here: 58.1 us
  Pallas kernels  55.7 us (96%)
  local copies, waits for them, and re-layouts  1.83 us (3%)
  between operations  0.64 us (1%)
    pallas_call x1, Pallas kernels, on_device(): pl.pallas_call(body, out_shape=(pltpu.VMEM((2, 32, 64), F32), pltpu.VMEM(...  55.7 us
    unnamed x3, local copies, waits for them, and re-layouts  1.83 us

profile of v7, /device:TPU:0, one launch (start us, length us, event | category | flops | bytes accessed | tf_op | source)
XLA Modules:
  0.0 58.1 jit_solution(5946804211259831863)
XLA Ops:
  0.6 55.7 %panel.1 = (f32[2,32,64]{2,1,0:T(8,128)S(1)}, f32[2,32,1024]{2,1,0:T(8,128)S(1)}, f32[1,4]{1,0:T(1,128)S(1)}) custom-call(f32[2,64,128]{2,1,0:T(8,128)} %upper_hbm.1, f32[2,64,64]{2,1,0:T(8,128)} %inverse_hbm.1, f32[2,32,64]{2,1,0:T(8,128)} %rhs_hbm.1, f32[2,64,16384]{2,1,0:T(8,128)} %trail_hbm.1, f32[2,32,1024]{2,1,0:T(8,128)} %trail_rhs_hbm.1, ...), custom_call_target="tpu_custom_call" | custom-call | tf_op jit(solution)/shard_map/panel/pallas_call | solution.py:402
  56.3 0.6 %copy.13 = f32[2,32,64]{2,1,0:T(8,128)} copy(f32[2,32,64]{2,1,0:T(8,128)S(1)} %get-tuple-element.9) | data formatting | bytes 32768
  56.9 0.5 copy.15
  57.4 0.7 %copy.14 = f32[2,32,1024]{2,1,0:T(8,128)} copy(f32[2,32,1024]{2,1,0:T(8,128)S(1)} %get-tuple-element.10) | data formatting | bytes 524288
